TPU v7x, 256 devices: a whole 4x4x8 slice. The times are simulated.
256 devices in a mesh: segment: 4 (over z_hi, core), ctx: 16 (over x, z_lo), dp: 4 (over y).
Axes of the slice: x: 4, y: 4, z: 8 (z_hi: 2, z_lo: 4; z = z_hi * 4 + z_lo), core: 2. Of those that a mesh axis runs over, the one named last changes fastest.
Arguments:
- qkv: bfloat16 [4, 4, 2560, 3, 2560], P('segment', 'dp', 'ctx'), may hold values from -24 to 24
- qk_gain: float32 [4, 2, 2560], P('segment'), may hold values from 1.5 to 2.5
- mod_weight: float32 [4, 256, 2560], P('segment'), may hold values from -0.375 to 0.375
- positions: int32 [4, 2560], P('dp', 'ctx'), may hold values from 0 to 75599
- timesteps: int32 [4, 4], P('segment', 'dp'), may hold values from 0 to 999
- cotangent: bfloat16 [4, 4, 2560, 2560], P('segment', 'dp', 'ctx'), may hold values from -6 to 6
Outputs:
- attn_out: bfloat16 [4, 4, 2560, 2560], P('segment', 'dp', 'ctx')
- gate_grad: float32 [4, 256, 2560], P('segment', ('ctx', 'dp'))
All inputs are finite; a program needn't handle non-finite values.
Results may differ from a plain program's by a relative error of at most 0.012.
Values may be sent and summed in bfloat16 or wider, within the bound.
No kernel may reach another device: no remote copies, remote signals or barrier semaphores. Data moves between devices by JAX's collectives and lax.ppermute only.
A program may use at most 128 MiB of HBM per device.

v0:
```python
import jax
import jax.numpy as jnp
from jax import lax
from jax.sharding import PartitionSpec as P

HEADS = 20
HEAD_DIM = 128
FREQS = 256
GRID_ROWS = 45
GRID_COLS = 80


def shifted(value, axis, by):
    length = lax.axis_size(axis)
    return lax.ppermute(value, axis, [(i, (i + by) % length) for i in range(length)])


def rope_tables(pos):
    half = HEAD_DIM // 2
    side = HEAD_DIM // 6
    first = half - 2 * side
    frame = (pos // (GRID_ROWS * GRID_COLS)).astype(jnp.float32)
    row = (pos // GRID_COLS % GRID_ROWS).astype(jnp.float32)
    col = (pos % GRID_COLS).astype(jnp.float32)
    pair = jnp.arange(half, dtype=jnp.int32)
    group = jnp.where(pair < first, 0, jnp.where(pair < first + side, 1, 2))
    offset = jnp.where(group == 0, 0, jnp.where(group == 1, first, first + side))
    pairs_in = jnp.where(group == 0, first, side).astype(jnp.float32)
    freq = 10000.0 ** (-(pair - offset).astype(jnp.float32) / pairs_in)
    coord = jnp.where(
        group[None, :] == 0,
        frame[:, None],
        jnp.where(group[None, :] == 1, row[:, None], col[:, None]),
    )
    angle = coord * freq[None, :]
    cosine = jnp.tile(jnp.concatenate([jnp.cos(angle), jnp.cos(angle)], axis=1), (1, HEADS))
    sine = jnp.tile(jnp.concatenate([jnp.sin(angle), jnp.sin(angle)], axis=1), (1, HEADS))
    return (cosine, sine)


def rotate(values, cosine, sine):
    count = values.shape[0]
    half = HEAD_DIM // 2
    shaped = values.reshape(count, HEADS, HEAD_DIM)
    turned = jnp.concatenate([-shaped[:, :, half:], shaped[:, :, :half]], axis=2).reshape(
        count, HEADS * HEAD_DIM
    )
    return values * cosine + turned * sine


def normalize(values, gain):
    mean_sq = jnp.mean(values * values, axis=-1, keepdims=True)
    return values * lax.rsqrt(mean_sq + 1e-06) * gain


def embed(step):
    count = FREQS // 2
    freq = 10000.0 ** (-jnp.arange(count, dtype=jnp.float32) / count)
    angle = step.astype(jnp.float32) * freq
    return jnp.concatenate([jnp.cos(angle), jnp.sin(angle)])


def head_major(rows):
    count = rows.shape[0]
    return rows.reshape(count, HEADS, HEAD_DIM).transpose(1, 0, 2)


def section_attention(block, gains, pos):
    count = block.shape[0]
    width = HEADS * HEAD_DIM
    cosine, sine = rope_tables(pos)
    queries = rotate(normalize(block[:, 0].astype(jnp.float32), gains[0]), cosine, sine).astype(
        jnp.bfloat16
    )
    keys = rotate(normalize(block[:, 1].astype(jnp.float32), gains[1]), cosine, sine).astype(
        jnp.bfloat16
    )
    queries = head_major(queries)
    keys = head_major(keys)
    values = head_major(block[:, 2])
    scale = 1.0 / HEAD_DIM**0.5

    def attend(carry, key_block, value_block):
        peak, total, accum = carry
        scores = (
            jnp.einsum("hqd,hkd->hqk", queries, key_block, preferred_element_type=jnp.float32)
            * scale
        )
        new_peak = jnp.maximum(peak, jnp.max(scores, axis=2))
        fade = jnp.exp(peak - new_peak)
        expo = jnp.exp(scores - new_peak[:, :, None])
        total = total * fade + jnp.sum(expo, axis=2)
        update = jnp.einsum(
            "hqk,hkd->hqd",
            expo.astype(jnp.bfloat16),
            value_block,
            preferred_element_type=jnp.float32,
        )
        return (new_peak, total, accum * fade[:, :, None] + update)

    start_state = (
        jnp.full((HEADS, count), -1e30, jnp.float32),
        jnp.zeros((HEADS, count), jnp.float32),
        jnp.zeros((HEADS, count, HEAD_DIM), jnp.float32),
    )
    key_heads = lax.all_gather(keys, "ctx", axis=1, tiled=True)
    value_heads = lax.all_gather(values, "ctx", axis=1, tiled=True)
    length = key_heads.shape[1]

    def step_block(index, state):
        begin = (index * 512).astype(jnp.int32)
        key_part = lax.dynamic_slice_in_dim(key_heads, begin, 512, 1)
        value_part = lax.dynamic_slice_in_dim(value_heads, begin, 512, 1)
        return attend(state, key_part, value_part)

    peak, total, accum = lax.fori_loop(0, length // 512, step_block, start_state)
    return (accum / total[:, :, None]).transpose(1, 0, 2).reshape(count, width)


def local(qkv, qk_gain, mod_weight, positions, timesteps, cotangent):
    source = shifted(qkv, "segment", 1)
    attn = section_attention(source[0, 0], qk_gain[0], positions[0])
    emb = embed(timesteps[0, 0])
    gate = jnp.dot(emb, mod_weight[0], precision=lax.Precision.HIGHEST)
    attn_out = (attn * gate).astype(jnp.bfloat16)[None, None]
    chan = jnp.sum(attn * cotangent[0, 0].astype(jnp.float32), axis=0)
    term = emb[:, None] * chan[None, :]
    gate_grad = lax.psum_scatter(term, ("ctx", "dp"), scatter_dimension=0, tiled=True)
    return (attn_out, gate_grad[None])


def solution(mesh):
    return jax.shard_map(
        local,
        mesh=mesh,
        in_specs=(
            P("segment", "dp", "ctx", None, None),
            P("segment", None, None),
            P("segment", None, None),
            P("dp", "ctx"),
            P("segment", "dp"),
            P("segment", "dp", "ctx", None),
        ),
        out_specs=(P("segment", "dp", "ctx", None), P("segment", ("ctx", "dp"), None)),
        check_vma=False,
    )
```

profile of v0, /device:TPU:8, one launch (start us, length us, event | category | flops | bytes accessed | tf_op | source)
XLA Modules:
  0.0 1465.4 jit_solution(14703225127395138899)
XLA Ops:
  10.9 38.4 %collective-permute-done = bf16[1,1,160,3,2560]{4,2,3,1,0:T(8,128)(2,1)S(1)} collective-permute-done((bf16[1,1,160,3,2560]{4,2,3,1,0:T(8,128)(2,1)}, bf16[1,1,160,3,2560]{4,2,3,1,0:T(8,128)(2,1)S(1)}, u32[]{:S(2)}, u32[]{:S(2)}) %collective-permute-start) | collective-permute-done | bytes 2457632 | tf_op jit(solution)/shard_map/ppermute | solution.py:15
  50.3 2.0 fusion.40
  52.4 2.6 reshape.231
  55.7 1.8 multiply_multiply_fusion.1
  57.5 2.5 slice_negate_fusion.1
  60.0 2.6 reshape.232
  62.7 1.8 multiply_multiply_fusion
  67.8 2.6 fusion.29
  73.0 2.3 copy.15
  79.3 295.2 %all-gather.3.cloned.1.call-done = bf16[20,2560,128]{2,1,0:T(8,128)(2,1)} async-done(((bf16[20,160,128]{2,1,0:T(8,128)(2,1)}), bf16[20,2560,128]{2,1,0:T(8,128)(2,1)}) %all-gather.3.cloned.1.call-update) | async-done | bytes 13107216 | tf_op jit(solution)/shard_map/all_gather | solution.py:106
  374.5 282.6 %all-gather.5.cloned.1.call-done = bf16[20,2560,128]{2,1,0:T(8,128)(2,1)} async-done(((bf16[20,160,128]{2,1,0:T(8,128)(2,1)}), bf16[20,2560,128]{2,1,0:T(8,128)(2,1)}) %all-gather.5.cloned.1.call-update) | async-done | bytes 13107216 | tf_op jit(solution)/shard_map/all_gather | solution.py:107
  657.1 77.8 %while.18 = (s32[]{:T(128)}, f32[20,160]{1,0:T(8,128)S(1)}, f32[20,160]{1,0:T(8,128)S(1)}, f32[20,160,128]{2,1,0:T(8,128)}, bf16[20,2560,128]{2,1,0:T(8,128)(2,1...) while((s32[]{:T(128)}, f32[20,160]{1,0:T(8,128)S(1)}, ...), condition=%wide.region_5.6_spmd.clone, body=%wide.region_2.5_spmd.clone.sunk | while | flops 853212800 | bytes 55419080 | solution.py:116
  657.1 5.5 bitcast_reduce_fusion.2
  662.7 4.3 fusion.52
  667.5 5.0 fusion.54
  672.5 5.5 bitcast_reduce_fusion.2
  678.0 4.3 fusion.52
  682.8 5.3 fusion.54
  688.1 5.5 bitcast_reduce_fusion.2
  693.7 4.3 fusion.52
  698.4 5.3 fusion.54
  703.7 5.5 bitcast_reduce_fusion.2
  709.3 4.3 fusion.52
  714.1 5.3 fusion.54
  719.4 5.5 bitcast_reduce_fusion.2
  724.9 4.3 fusion.52
  729.7 5.3 fusion.54
  735.1 2.9 multiply_reduce_fusion
  743.1 3.3 fusion.25
  746.4 2.7 reshape.230
  749.1 2.4 multiply_convert_fusion
  751.5 705.8 %all-reduce.3.cloned.1.call-done = f32[256,2560]{1,0:T(8,128)} async-done(((f32[256,2560]{1,0:T(8,128)}), f32[256,2560]{1,0:T(8,128)}) %all-reduce.3.cloned.1.call-update) | async-done | bytes 2621456
  (76 shorter events, 22.9 us)
Async XLA Ops:
  7.2 734.5 %copy-start = (f32[1,256,2560]{2,1,0:T(8,128)S(1)}, f32[1,256,2560]{2,1,0:T(8,128)}, u32[]{:S(2)}) copy-start(f32[1,256,2560]{2,1,0:T(8,128)} %param.10) | copy-start | bytes 7864324
  7.2 367.3 %all-gather.3.cloned.1.call-start = ((), (), s32[]{:S(2)}) async-start(), calls=%async_computation | async-start | bytes 13926400 | tf_op jit(solution)/shard_map/all_gather | solution.py:106
  7.2 42.1 %collective-permute-start = (bf16[1,1,160,3,2560]{4,2,3,1,0:T(8,128)(2,1)}, bf16[1,1,160,3,2560]{4,2,3,1,0:T(8,128)(2,1)S(1)}, u32[]{:S(2)}, u32[]{:S(2)}) collective-permute-start(bf16[1,1,160,3,2560]{4,2,3,1,0:T(8,128)(2,1)} %param.8), channel_id=1, source_target_pairs={{0,64},{64,128},{128,192},{192,0},{1,65},{65,129},{129,193},{193,1... | collective-permute-start | bytes 7372808 | tf_op jit(solution)/shard_map/ppermute | solution.py:15
  62.7 2.5 copy-start.8
  64.5 1.5 copy-start.3
  64.5 2.1 copy-start.4
  64.5 2.7 copy-start.5
  64.5 3.3 copy-start.6
  71.5 585.7 %all-gather.5.cloned.1.call-start = ((), (), s32[]{:S(2)}) async-start(), calls=%async_computation.1 | async-start | bytes 13926400 | tf_op jit(solution)/shard_map/all_gather | solution.py:107
  73.0 2.6 copy-start.7
  75.3 1382.1 %all-reduce.3.cloned.1.call-start = ((), (), s32[]{:S(2)}) async-start(), calls=%async_computation.2 | async-start | bytes 5242880
  662.7 4.8 copy-start.1
  678.0 4.8 copy-start.1
  693.7 4.8 copy-start.1
  709.3 4.8 copy-start.1
  724.9 4.8 copy-start.1
  739.7 0.7 copy-start.9
  741.6 1.4 copy-start.2
Sparse Core Ops, SparseCore 0:
  71.6 302.8 all-gather.2
  376.3 280.8 all-gather.4
  739.9 717.4 all-reduce.2
where the time goes:
time: 1470 us
  waiting for transfers between devices  1320 us (90%)
  matrix products  55.2 us (4%)
  other arithmetic  47.9 us (3%)
  local copies, waits for them, and re-layouts  24.4 us (2%)
  between operations  15.3 us (1%)
    unnamed x4, waiting for transfers between devices  706 us
    all_gather x1, waiting for transfers between devices, section_attention(): key_heads = lax.all_gather(keys, 'ctx', axis=1, tiled=True)  295 us
    all_gather x1, waiting for transfers between devices, section_attention(): value_heads = lax.all_gather(values, 'ctx', axis=1, tiled=True)  283 us
    ppermute x1, waiting for transfers between devices, shifted(): lax.ppermute(value, axis, [(i, (i + by) % length) for i in range(length)])  38.4 us
  transfers between devices with their start and end apart: 4, of which 4 were waited for; matrix products, arithmetic and copies ran while one was open for 1% of the time, Pallas kernels for 0%

commit v1 on v0

v1 whole, which is shorter than its diff:
```python
import functools

import jax
import jax.numpy as jnp
from jax import lax
from jax.experimental import pallas as pl
from jax.experimental.pallas import tpu as pltpu
from jax.sharding import PartitionSpec as P

HEADS = 20
HEAD_DIM = 128
FREQS = 256
GRID_ROWS = 45
GRID_COLS = 80
SIDE = 4
GROUP = HEADS // SIDE
TOK = 160
ROWS = SIDE * TOK
WIDTH = HEADS * HEAD_DIM
TILE = 320
EXP_SCALE = 1.4426950408889634 / HEAD_DIM**0.5
VMEM = pltpu.CompilerParams(vmem_limit_bytes=56 * 1024 * 1024)
SMEM_SPEC = pl.BlockSpec(memory_space=pltpu.SMEM)
VMEM_SPEC = pl.BlockSpec(memory_space=pltpu.VMEM)


def along_z(value, by):
    pairs = [(i, i // SIDE * SIDE + (i + by) % SIDE) for i in range(SIDE * SIDE)]
    return lax.ppermute(value, "ctx", pairs)


def along_x(value, by):
    pairs = [(i, (i + SIDE * by) % (SIDE * SIDE)) for i in range(SIDE * SIDE)]
    return lax.ppermute(value, "ctx", pairs)


def along_dp(value, by):
    return lax.ppermute(value, "dp", [(i, (i + by) % SIDE) for i in range(SIDE)])


def home(value, by):
    count = SIDE * SIDE
    pairs = []
    for seg in range(SIDE):
        for i in range(count):
            target = (seg + 1) % SIDE * count + i // SIDE * SIDE + (i + by) % SIDE
            pairs.append((seg * count + i, target))
    return lax.ppermute(value, ("segment", "ctx"), pairs)


def rope_tables(pos):
    half = HEAD_DIM // 2
    side = HEAD_DIM // 6
    first = half - 2 * side
    frame = (pos // (GRID_ROWS * GRID_COLS)).astype(jnp.float32)
    row = (pos // GRID_COLS % GRID_ROWS).astype(jnp.float32)
    col = (pos % GRID_COLS).astype(jnp.float32)
    pair = jnp.arange(half, dtype=jnp.int32)
    group = jnp.where(pair < first, 0, jnp.where(pair < first + side, 1, 2))
    offset = jnp.where(group == 0, 0, jnp.where(group == 1, first, first + side))
    pairs_in = jnp.where(group == 0, first, side).astype(jnp.float32)
    freq = 10000.0 ** (-(pair - offset).astype(jnp.float32) / pairs_in)
    coord = jnp.where(
        group[None, :] == 0,
        frame[:, None],
        jnp.where(group[None, :] == 1, row[:, None], col[:, None]),
    )
    angle = coord * freq[None, :]
    cosine = jnp.concatenate([jnp.cos(angle), jnp.cos(angle)], axis=1)
    sine = jnp.concatenate([-jnp.sin(angle), jnp.sin(angle)], axis=1)
    return (cosine, sine)


def call(kernel, out_shape, flops, moved, *operands, smem=1):
    specs = [SMEM_SPEC] * smem + [VMEM_SPEC] * (len(operands) - smem)
    return pl.pallas_call(
        kernel,
        out_shape=out_shape,
        in_specs=specs,
        out_specs=jax.tree.map(lambda _: VMEM_SPEC, out_shape),
        compiler_params=VMEM,
        cost_estimate=pl.CostEstimate(flops=flops, bytes_accessed=moved, transcendentals=0),
    )(*operands)


def column(index):
    return pl.ds(pl.multiple_of(index * HEAD_DIM, HEAD_DIM), HEAD_DIM)


def prep_kernel(z_ref, qkv_ref, gain_ref, cos_ref, sin_ref, *outs):
    z = z_ref[0]
    cosine = cos_ref[...]
    sine = sin_ref[...]
    for part in range(2):
        total = jnp.zeros((TOK, HEAD_DIM), jnp.float32)
        for head in range(HEADS):
            x = qkv_ref[part, :, head * HEAD_DIM : (head + 1) * HEAD_DIM].astype(jnp.float32)
            total = total + x * x
        mean_sq = jnp.sum(total, axis=1, keepdims=True) / WIDTH
        inverse = lax.rsqrt(mean_sq + 1e-06)
        for step in range(SIDE):
            first = lax.rem(z + step, SIDE) * GROUP
            for head in range(GROUP):
                cols = column(first + head)
                x = qkv_ref[part, :, cols].astype(jnp.float32)
                y = x * inverse * gain_ref[part : part + 1, cols]
                turned = pltpu.roll(y, HEAD_DIM // 2, 1)
                y = y * cosine + turned * sine
                outs[step][part * GROUP + head] = y.astype(jnp.bfloat16)
    for step in range(SIDE):
        first = lax.rem(z + step, SIDE) * GROUP
        for head in range(GROUP):
            outs[step][2 * GROUP + head] = qkv_ref[2, :, column(first + head)]


def split_kernel(x_ref, r0, r1, r2, r3, *outs):
    x = x_ref[0]
    last = GROUP - 1
    for j, r in enumerate((r0, r1, r2, r3)):
        rows = pl.ds(j * TOK, TOK)
        for step in range(SIDE):
            head = lax.rem(x + step, SIDE)
            out = outs[step]
            out[0, rows] = r[head]
            out[1, rows] = r[GROUP + head]
            out[2, rows] = r[2 * GROUP + head]
            out[3, rows] = r[GROUP + last]
            out[4, rows] = r[2 * GROUP + last]
        outs[SIDE][rows] = r[last]


def attend(q, blocks, keys_at, values_at):
    nt = (((1,), (1,)), ((), ()))
    scores = [
        lax.dot_general(q, b[keys_at], nt, preferred_element_type=jnp.float32) for b in blocks
    ]
    peak = functools.reduce(jnp.maximum, [jnp.max(s, axis=1, keepdims=True) for s in scores])
    expo = [jnp.exp2((s - peak) * EXP_SCALE) for s in scores]
    total = sum(jnp.sum(e, axis=1, keepdims=True) for e in expo)
    accum = sum(
        jnp.dot(e.astype(jnp.bfloat16), b[values_at], preferred_element_type=jnp.float32)
        for e, b in zip(expo, blocks, strict=True)
    )
    return (accum / total).astype(jnp.bfloat16)


def attention_kernel(t0, t1, t2, t3, shared_ref, *outs):
    blocks = (t0, t1, t2, t3)

    def tile(i, _):
        rows = pl.ds(pl.multiple_of(i * TILE, TILE), TILE)
        for step in range(SIDE):
            outs[step][rows] = attend(blocks[step][0, rows], blocks, 1, 2)
        outs[SIDE][rows] = attend(shared_ref[rows], blocks, 3, 4)
        return 0

    lax.fori_loop(0, ROWS // TILE, tile, 0)


def join_kernel(x_ref, o0, o1, o2, o3, shared_ref, *outs):
    x = x_ref[0]
    for j in range(SIDE):
        rows = pl.ds(j * TOK, TOK)
        for step, o in enumerate((o0, o1, o2, o3)):
            outs[j][:, column(lax.rem(x + step, SIDE))] = o[rows]
        outs[j][:, (GROUP - 1) * HEAD_DIM :] = shared_ref[rows]


def finish_kernel(z_ref, a0, a1, a2, a3, gate_ref, cot_ref, out_ref, chan_ref):
    z = z_ref[0]
    wide = GROUP * HEAD_DIM
    for step, a in enumerate((a0, a1, a2, a3)):
        cols = pl.ds(pl.multiple_of(lax.rem(z + step, SIDE) * wide, HEAD_DIM), wide)
        attn = a[...].astype(jnp.float32)
        out_ref[:, cols] = (attn * gate_ref[:, cols]).astype(jnp.bfloat16)
        chan_ref[:, cols] = jnp.sum(
            attn * cot_ref[:, cols].astype(jnp.float32), axis=0, keepdims=True
        )


def shape(dims, dtype=jnp.bfloat16):
    return jax.ShapeDtypeStruct(dims, dtype)


def frequencies():
    count = FREQS // 2
    return 10000.0 ** (-jnp.arange(count, dtype=jnp.float32) / count)


def embed(step):
    angle = step.astype(jnp.float32) * frequencies()
    return jnp.concatenate([jnp.cos(angle), jnp.sin(angle)])


def local(qkv, qk_gain, mod_weight, positions, timesteps, cotangent):
    ctx = lax.axis_index("ctx").astype(jnp.int32)
    x = (ctx // SIDE)[None]
    z = (ctx % SIDE)[None]
    gains = lax.ppermute(qk_gain[0], "segment", [((i + 1) % SIDE, i) for i in range(SIDE)])
    cosine, sine = rope_tables(positions[0])
    parts = qkv[0, 0].transpose(1, 0, 2)
    sent = call(
        prep_kernel,
        [shape((3 * GROUP, TOK, HEAD_DIM))] * SIDE,
        10_000_000,
        5_000_000,
        z,
        parts,
        gains,
        cosine,
        sine,
    )
    blocks = [sent[0]] + [along_z(sent[k], k) for k in (1, 2, 3)]
    split = call(
        split_kernel,
        [shape((GROUP, ROWS, HEAD_DIM))] * SIDE + [shape((ROWS, HEAD_DIM))],
        0,
        6_000_000,
        x,
        *blocks,
    )
    held = [split[0]] + [along_x(split[m], m) for m in (1, 2, 3)]
    heads = call(
        attention_kernel,
        [shape((ROWS, HEAD_DIM))] * (SIDE + 1),
        4_200_000_000,
        5_000_000,
        *held,
        split[SIDE],
        smem=0,
    )
    back = [heads[0]] + [along_x(heads[m], SIDE - m) for m in (1, 2, 3)]
    joined = call(
        join_kernel,
        [shape((TOK, GROUP * HEAD_DIM))] * SIDE,
        0,
        2_000_000,
        x,
        *back,
        heads[SIDE],
    )
    at_home = [home(joined[k], SIDE - k) for k in range(SIDE)]

    step = timesteps[0, 0]
    emb = embed(step)
    gate = jnp.dot(emb, mod_weight[0], precision=lax.Precision.HIGHEST)
    attn_out, chan = call(
        finish_kernel,
        [shape((TOK, WIDTH)), shape((1, WIDTH), jnp.float32)],
        2_000_000,
        3_000_000,
        z,
        *at_home,
        gate[None],
        cotangent[0, 0],
    )
    chan = chan.reshape(HEADS, HEAD_DIM)
    chan = chan + along_x(chan, 1) + along_x(chan, 2) + along_x(chan, 3)
    chan = chan + along_z(chan, 1) + along_z(chan, 2) + along_z(chan, 3)
    when = jnp.full((1, HEAD_DIM), step.astype(jnp.float32))
    mine = jnp.concatenate([chan, when])
    clips = [mine] + [along_dp(mine, k) for k in (1, 2, 3)]

    rows = FREQS // (SIDE * SIDE * SIDE)
    index = (ctx * SIDE + lax.axis_index("dp").astype(jnp.int32)) * rows
    freq = lax.dynamic_slice_in_dim(jnp.tile(frequencies(), 2), index, rows)
    grad = 0.0
    for clip in clips:
        angle = clip[HEADS, 0] * freq
        part = jnp.where(index < FREQS // 2, jnp.cos(angle), jnp.sin(angle))
        grad = grad + part[:, None] * clip[:HEADS].reshape(1, WIDTH)
    return (attn_out[None, None], grad[None])


def solution(mesh):
    return jax.shard_map(
        local,
        mesh=mesh,
        in_specs=(
            P("segment", "dp", "ctx", None, None),
            P("segment", None, None),
            P("segment", None, None),
            P("dp", "ctx"),
            P("segment", "dp"),
            P("segment", "dp", "ctx", None),
        ),
        out_specs=(P("segment", "dp", "ctx", None), P("segment", ("ctx", "dp"), None)),
        check_vma=False,
    )
```

time: 1470 us -> 198 us (0.13)
  waiting for transfers between devices: 1320 us -> 102 us
  matrix products: 55.2 us -> 1.94 us
  starting transfers between devices: 0.38 us -> 51.5 us
  other arithmetic: 47.9 us -> 6.23 us
  Pallas kernels: 0 us -> 27.9 us
  local copies, waits for them, and re-layouts: 24.4 us -> 4.87 us
    unnamed x4 -> x0, waiting for transfers between devices: 706 us -> none
    all_gather x2 -> x0, waiting for transfers between devices: 578 us -> none  [the longest x1 295 us: section_attention(): key_heads = lax.all_gather(keys, 'ctx', axis=1, tiled=True)]
    ppermute x1 -> x23, waiting for transfers between devices: 38.4 us -> 102 us  [the longest x9 45.1 us: along_x(): return lax.ppermute(value, 'ctx', pairs)]
    dot_general x10 -> x0, matrix products: 53.9 us -> none  [the longest x5 27.6 us: attend(): jnp.einsum('hqd,hkd->hqk', queries, key_block, preferred_element_type=jnp...]
    ppermute x1 -> x23, starting transfers between devices: 0.08 us -> 51.5 us  [the longest x4 17.7 us: home(): return lax.ppermute(value, ('segment', 'ctx'), pairs)]
    pallas_call x0 -> x5, Pallas kernels: none -> 27.9 us  [call(): pl.pallas_call(kernel, out_shape=out_shape, in_specs=specs, out_specs=jax...]
    reduce_sum x7 -> x0, other arithmetic: 25.3 us -> none  [the longest x5 21.5 us: attend(): total = total * fade + jnp.sum(expo, axis=2)]
  transfers between devices with their start and end apart: 4 -> 23, of which waited for: 4 -> 16; matrix products, arithmetic and copies ran while one was open for 1% -> 3% of each run, Pallas kernels for 0% -> 0%
where the time goes in v1:
time: 198 us; the launch traced here: 196 us
  waiting for transfers between devices  102 us (52%)
  starting transfers between devices  51.5 us (26%)
  Pallas kernels  27.9 us (14%)
  other arithmetic  6.23 us (3%)
  local copies, waits for them, and re-layouts  4.87 us (2%)
    ppermute x9, waiting for transfers between devices, along_x(): return lax.ppermute(value, 'ctx', pairs)  45.1 us
    ppermute x6, waiting for transfers between devices, along_z(): return lax.ppermute(value, 'ctx', pairs)  42.9 us
    pallas_call x5, Pallas kernels, call(): pl.pallas_call(kernel, out_shape=out_shape, in_specs=specs, out_specs=jax...  27.9 us
    ppermute x4, starting transfers between devices, home(): return lax.ppermute(value, ('segment', 'ctx'), pairs)  17.7 us
    ppermute x4, waiting for transfers between devices, home(): return lax.ppermute(value, ('segment', 'ctx'), pairs)  13.2 us
    ppermute x9, starting transfers between devices, along_x(): return lax.ppermute(value, 'ctx', pairs)  12.8 us
    ppermute x6, starting transfers between devices, along_z(): return lax.ppermute(value, 'ctx', pairs)  9.26 us
    ppermute x1, starting transfers between devices, local(): lax.ppermute(qk_gain[0], 'segment', [((i + 1) % SIDE, i) for i in range(S...  6.71 us
  transfers between devices with their start and end apart: 23, of which 16 were waited for; matrix products, arithmetic and copies ran while one was open for 3% of the time, Pallas kernels for 0%

profile of v1, /device:TPU:8, one launch (start us, length us, event | category | flops | bytes accessed | tf_op | source)
XLA Modules:
  0.0 196.2 jit_solution(7644259920816154818)
XLA Ops:
  0.6 6.7 %collective-permute-start = (f32[2,2560]{1,0:T(2,128)}, f32[2,2560]{1,0:T(2,128)S(1)}, u32[]{:S(2)}, u32[]{:S(2)}) collective-permute-start(f32[2,2560]{1,0:T(2,128)} %bitcast.42), channel_id=1, source_target_pairs={{64,0},{128,64},{192,128},{0,192},{65,1},{129,65},{193,129},{1,193... | collective-permute-start | bytes 61448 | tf_op jit(solution)/shard_map/ppermute | solution.py:199
  10.6 4.6 %shard_map.77 = (bf16[15,160,128]{2,1,0:T(8,128)(2,1)}, bf16[15,160,128]{2,1,0:T(8,128)(2,1)}, bf16[15,160,128]{2,1,0:T(8,128)(2,1)}, bf16[15,160,128]{2,1,0:T(8,128)(2,1)}) custom-call(s32[1]{0:T(128)} %bitcast.z_ref, bf16[3,160,2560]{2,1,0:T(8,128)(2,1)} %bitcast.31, f32[2,2560]{1,0:T(2,128)} %copy-done.9, f32[160,128]{1,0:T(8,128)} %get-tuple-element.58.cos_ref, ...), custom_call_target="tpu_custom_call" | custom-call | flops 10000000 | bytes 5000000 | tf_op jit(solution)/shard_map/pallas_call | solution.py:76
  16.3 1.5 collective-permute-start.2
  17.8 1.9 collective-permute-start.3
  19.7 14.5 %collective-permute-done.1.r1 = bf16[15,160,128]{2,1,0:T(8,128)(2,1)S(1)} collective-permute-done((bf16[15,160,128]{2,1,0:T(8,128)(2,1)}, bf16[15,160,128]{2,1,0:T(8,128)(2,1)S(1)}, u32[]{:S(2)}, u32[]{:S(2)}) %collective-permute-start.1) | collective-permute-done | bytes 614432 | tf_op jit(solution)/shard_map/ppermute | solution.py:29
  34.2 25.2 %collective-permute-done.2.r2 = bf16[15,160,128]{2,1,0:T(8,128)(2,1)} collective-permute-done((bf16[15,160,128]{2,1,0:T(8,128)(2,1)}, bf16[15,160,128]{2,1,0:T(8,128)(2,1)}, u32[]{:S(2)}, u32[]{:S(2)}) %collective-permute-start.2) | collective-permute-done | bytes 614432 | tf_op jit(solution)/shard_map/ppermute | solution.py:29
  59.3 3.5 %shard_map.78 = (bf16[5,640,128]{2,1,0:T(8,128)(2,1)}, bf16[5,640,128]{2,1,0:T(8,128)(2,1)}, bf16[5,640,128]{2,1,0:T(8,128)(2,1)}, bf16[5,640,128]{2,1,0:T(8,128)(2,1)}, bf16[640,128]{1,0:T(8,128)(2,1)}) custom-call(s32[1]{0:T(128)} %bitcast.1.x_ref, bf16[15,160,128]{2,1,0:T(8,128)(2,1)} %get-tuple-element.22.r0, bf16[15,160,128]{2,1,0:T(8,128)(2,1)} %copy-done.1, ...), custom_call_target="tpu_custom_call" | custom-call | bytes 6000000 | tf_op jit(solution)/shard_map/pallas_call | solution.py:76
  62.9 1.5 collective-permute-start.4
  64.4 2.7 %collective-permute-start.5 = (bf16[5,640,128]{2,1,0:T(8,128)(2,1)}, bf16[5,640,128]{2,1,0:T(8,128)(2,1)S(1)}, u32[]{:S(2)}, u32[]{:S(2)}) collective-permute-start(bf16[5,640,128]{2,1,0:T(8,128)(2,1)} %get-tuple-element.28), channel_id=1, source_target_pairs={{0,32},{4,36},{8,40},{12,44},{16,48},{20,52},{24,56},{28,60},{32,0... | collective-permute-start | bytes 2457608 | tf_op jit(solution)/shard_map/ppermute | solution.py:34
  67.1 1.4 collective-permute-start.6
  69.2 15.3 %collective-permute-done.4.t1 = bf16[5,640,128]{2,1,0:T(8,128)(2,1)S(1)} collective-permute-done((bf16[5,640,128]{2,1,0:T(8,128)(2,1)}, bf16[5,640,128]{2,1,0:T(8,128)(2,1)S(1)}, u32[]{:S(2)}, u32[]{:S(2)}) %collective-permute-start.4) | collective-permute-done | bytes 819232 | tf_op jit(solution)/shard_map/ppermute | solution.py:34
  84.5 18.1 %collective-permute-done.5.t2 = bf16[5,640,128]{2,1,0:T(8,128)(2,1)S(1)} collective-permute-done((bf16[5,640,128]{2,1,0:T(8,128)(2,1)}, bf16[5,640,128]{2,1,0:T(8,128)(2,1)S(1)}, u32[]{:S(2)}, u32[]{:S(2)}) %collective-permute-start.5) | collective-permute-done | bytes 819232 | tf_op jit(solution)/shard_map/ppermute | solution.py:34
  103.8 14.9 %shard_map.79 = (bf16[640,128]{1,0:T(8,128)(2,1)}, bf16[640,128]{1,0:T(8,128)(2,1)}, bf16[640,128]{1,0:T(8,128)(2,1)}, bf16[640,128]{1,0:T(8,128)(2,1)}, bf16[640,128]{1,0:T(8,128)(2,1)}) custom-call(bf16[5,640,128]{2,1,0:T(8,128)(2,1)} %get-tuple-element.26.t0, bf16[5,640,128]{2,1,0:T(8,128)(2,1)} %copy-done.10, bf16[5,640,128]{2,1,0:T(8,128)(2,1)} %copy-done.11, ...), custom_call_target="tpu_custom_call" | custom-call | flops 4200000000 | bytes 5000000 | tf_op jit(solution)/shard_map/pallas_call | solution.py:76
  118.6 2.0 %collective-permute-start.7 = (bf16[640,128]{1,0:T(8,128)(2,1)}, bf16[640,128]{1,0:T(8,128)(2,1)S(1)}, u32[]{:S(2)}, u32[]{:S(2)}) collective-permute-start(bf16[640,128]{1,0:T(8,128)(2,1)} %get-tuple-element.32), channel_id=1, source_target_pairs={{0,48},{4,52},{8,56},{12,60},{16,0},{20,4},{24,8},{28,12},{32,16},... | collective-permute-start | bytes 491528 | tf_op jit(solution)/shard_map/ppermute | solution.py:34
  122.5 5.6 %collective-permute-done.7.o1 = bf16[640,128]{1,0:T(8,128)(2,1)S(1)} collective-permute-done((bf16[640,128]{1,0:T(8,128)(2,1)}, bf16[640,128]{1,0:T(8,128)(2,1)S(1)}, u32[]{:S(2)}, u32[]{:S(2)}) %collective-permute-start.7) | collective-permute-done | bytes 163872 | tf_op jit(solution)/shard_map/ppermute | solution.py:34
  128.1 1.4 collective-permute-done.8.o2
  129.4 2.1 %collective-permute-done.9.o3 = bf16[640,128]{1,0:T(8,128)(2,1)S(1)} collective-permute-done((bf16[640,128]{1,0:T(8,128)(2,1)}, bf16[640,128]{1,0:T(8,128)(2,1)S(1)}, u32[]{:S(2)}, u32[]{:S(2)}) %collective-permute-start.9) | collective-permute-done | bytes 163872 | tf_op jit(solution)/shard_map/ppermute | solution.py:34
  132.2 2.3 %shard_map.80 = (bf16[160,640]{1,0:T(8,128)(2,1)}, bf16[160,640]{1,0:T(8,128)(2,1)}, bf16[160,640]{1,0:T(8,128)(2,1)}, bf16[160,640]{1,0:T(8,128)(2,1)}) custom-call(s32[1]{0:T(128)} %bitcast.1.x_ref, bf16[640,128]{1,0:T(8,128)(2,1)} %get-tuple-element.31.o0, bf16[640,128]{1,0:T(8,128)(2,1)} %copy-done.6, bf16[640,128]{1,0:T(8,128)(2,1)} %copy-done.7, ...), custom_call_target="tpu_custom_call" | custom-call | bytes 2000000 | tf_op jit(solution)/shard_map/pallas_call | solution.py:76
  134.4 13.7 %collective-permute-start.11 = (bf16[160,640]{1,0:T(8,128)(2,1)}, bf16[160,640]{1,0:T(8,128)(2,1)S(1)}, u32[]{:S(2)}, u32[]{:S(2)}) collective-permute-start(bf16[160,640]{1,0:T(8,128)(2,1)} %get-tuple-element.37), channel_id=1, source_target_pairs={{0,76},{4,64},{8,68},{12,72},{16,92},{20,80},{24,84},{28,88},{32,1... | collective-permute-start | bytes 614408 | tf_op jit(solution)/shard_map/ppermute | solution.py:48
  148.2 2.1 %collective-permute-start.12 = (bf16[160,640]{1,0:T(8,128)(2,1)}, bf16[160,640]{1,0:T(8,128)(2,1)S(1)}, u32[]{:S(2)}, u32[]{:S(2)}) collective-permute-start(bf16[160,640]{1,0:T(8,128)(2,1)} %get-tuple-element.38), channel_id=1, source_target_pairs={{0,72},{4,76},{8,64},{12,68},{16,88},{20,92},{24,80},{28,84},{32,1... | collective-permute-start | bytes 614408 | tf_op jit(solution)/shard_map/ppermute | solution.py:48
  150.2 1.9 collective-permute-start.13
  152.2 1.9 fusion.gate_ref
  154.1 12.1 %collective-permute-done.11.a1 = bf16[160,640]{1,0:T(8,128)(2,1)S(1)} collective-permute-done((bf16[160,640]{1,0:T(8,128)(2,1)}, bf16[160,640]{1,0:T(8,128)(2,1)S(1)}, u32[]{:S(2)}, u32[]{:S(2)}) %collective-permute-start.11) | collective-permute-done | bytes 204832 | tf_op jit(solution)/shard_map/ppermute | solution.py:48
  168.1 2.6 %shard_map.81 = (bf16[160,2560]{1,0:T(8,128)(2,1)}, f32[1,2560]{1,0:T(1,128)}) custom-call(s32[1]{0:T(128)} %bitcast.z_ref, bf16[160,640]{1,0:T(8,128)(2,1)} %copy-done.2, bf16[160,640]{1,0:T(8,128)(2,1)} %copy-done.3, bf16[160,640]{1,0:T(8,128)(2,1)} %copy-done.4, bf16[160,640]{1,0:T(8,128)(2,1)} %copy-done.5, f32[1,2560]{1,0:T(1,128)} %fusion.gate_ref, ...), custom_call_target="tpu_custom_call" | custom-call | flops 2000000 | bytes 3000000 | tf_op jit(solution)/shard_map/pallas_call | solution.py:76
  171.5 2.2 %collective-permute-start.15 = (f32[20,128]{1,0:T(8,128)S(1)}, f32[20,128]{1,0:T(8,128)S(1)}, u32[]{:S(2)}, u32[]{:S(2)}) collective-permute-start(f32[20,128]{1,0:T(8,128)S(1)} %bitcast.35), channel_id=1, source_target_pairs={{0,32},{4,36},{8,40},{12,44},{16,48},{20,52},{24,56},{28,60},{32,0... | collective-permute-start | bytes 30728 | tf_op jit(solution)/shard_map/ppermute | solution.py:34
  174.8 1.7 collective-permute-done.14
  177.4 2.4 %collective-permute-start.17 = (f32[20,128]{1,0:T(8,128)S(1)}, f32[20,128]{1,0:T(8,128)S(1)}, u32[]{:S(2)}, u32[]{:S(2)}) collective-permute-start(f32[20,128]{1,0:T(8,128)S(1)} %add_add_fusion.1), channel_id=1, source_target_pairs={{0,4},{4,8},{8,12},{12,0},{16,20},{20,24},{24,28},{28,16},{32,36},... | collective-permute-start | bytes 30728 | tf_op jit(solution)/shard_map/ppermute | solution.py:29
  179.9 2.0 %collective-permute-start.18 = (f32[20,128]{1,0:T(8,128)S(1)}, f32[20,128]{1,0:T(8,128)S(1)}, u32[]{:S(2)}, u32[]{:S(2)}) collective-permute-start(f32[20,128]{1,0:T(8,128)S(1)} %add_add_fusion.1), channel_id=1, source_target_pairs={{0,8},{4,12},{8,0},{12,4},{16,24},{20,28},{24,16},{28,20},{32,40},... | collective-permute-start | bytes 30728 | tf_op jit(solution)/shard_map/ppermute | solution.py:29
  183.0 1.5 collective-permute-done.18
  185.6 1.6 collective-permute-start.20
  188.2 2.4 %collective-permute-start.22 = (f32[21,128]{1,0:T(8,128)S(1)}, f32[21,128]{1,0:T(8,128)S(1)}, u32[]{:S(2)}, u32[]{:S(2)}) collective-permute-start(f32[21,128]{1,0:T(8,128)S(1)} %concatenate.15), channel_id=1, source_target_pairs={{0,3},{1,0},{2,1},{3,2},{4,7},{5,4},{6,5},{7,6},{8,11},{9,8},{10,9... | collective-permute-start | bytes 32264 | tf_op jit(solution)/shard_map/ppermute | solution.py:38
  193.5 2.0 broadcast_select_fusion.2
  (71 shorter events, 19.5 us)
Async XLA Ops:
  0.6 151.5 %copy-start = (f32[1,256,2560]{2,1,0:T(8,128)S(1)}, f32[1,256,2560]{2,1,0:T(8,128)}, u32[]{:S(2)}) copy-start(f32[1,256,2560]{2,1,0:T(8,128)} %param.8) | copy-start | bytes 7864324
  0.6 9.4 %collective-permute-start = (f32[2,2560]{1,0:T(2,128)}, f32[2,2560]{1,0:T(2,128)S(1)}, u32[]{:S(2)}, u32[]{:S(2)}) collective-permute-start(f32[2,2560]{1,0:T(2,128)} %bitcast.42), channel_id=1, source_target_pairs={{64,0},{128,64},{192,128},{0,192},{65,1},{129,65},{193,129},{1,193... | collective-permute-start | bytes 61448 | tf_op jit(solution)/shard_map/ppermute | solution.py:199
  15.3 18.9 %collective-permute-start.1 = (bf16[15,160,128]{2,1,0:T(8,128)(2,1)}, bf16[15,160,128]{2,1,0:T(8,128)(2,1)S(1)}, u32[]{:S(2)}, u32[]{:S(2)}) collective-permute-start(bf16[15,160,128]{2,1,0:T(8,128)(2,1)} %get-tuple-element.23), channel_id=1, source_target_pairs={{0,4},{4,8},{8,12},{12,0},{16,20},{20,24},{24,28},{28,16},{32,36},... | collective-permute-start | bytes 1843208 | tf_op jit(solution)/shard_map/ppermute | solution.py:29
  16.3 43.0 %collective-permute-start.2 = (bf16[15,160,128]{2,1,0:T(8,128)(2,1)}, bf16[15,160,128]{2,1,0:T(8,128)(2,1)}, u32[]{:S(2)}, u32[]{:S(2)}) collective-permute-start(bf16[15,160,128]{2,1,0:T(8,128)(2,1)} %get-tuple-element.24), channel_id=1, source_target_pairs={{0,8},{4,12},{8,0},{12,4},{16,24},{20,28},{24,16},{28,20},{32,40},... | collective-permute-start | bytes 1843208 | tf_op jit(solution)/shard_map/ppermute | solution.py:29
  17.8 41.5 %collective-permute-start.3 = (bf16[15,160,128]{2,1,0:T(8,128)(2,1)}, bf16[15,160,128]{2,1,0:T(8,128)(2,1)}, u32[]{:S(2)}, u32[]{:S(2)}) collective-permute-start(bf16[15,160,128]{2,1,0:T(8,128)(2,1)} %get-tuple-element.25), channel_id=1, source_target_pairs={{0,12},{4,0},{8,4},{12,8},{16,28},{20,16},{24,20},{28,24},{32,44},... | collective-permute-start | bytes 1843208 | tf_op jit(solution)/shard_map/ppermute | solution.py:29
  34.2 25.2 %copy-start.1 = (bf16[15,160,128]{2,1,0:T(8,128)(2,1)}, bf16[15,160,128]{2,1,0:T(8,128)(2,1)S(1)}, u32[]{:S(2)}) copy-start(bf16[15,160,128]{2,1,0:T(8,128)(2,1)S(1)} %collective-permute-done.1.r1) | copy-start | bytes 1843204
  62.9 21.6 %collective-permute-start.4 = (bf16[5,640,128]{2,1,0:T(8,128)(2,1)}, bf16[5,640,128]{2,1,0:T(8,128)(2,1)S(1)}, u32[]{:S(2)}, u32[]{:S(2)}) collective-permute-start(bf16[5,640,128]{2,1,0:T(8,128)(2,1)} %get-tuple-element.27), channel_id=1, source_target_pairs={{0,16},{4,20},{8,24},{12,28},{16,32},{20,36},{24,40},{28,44},{32,4... | collective-permute-start | bytes 2457608 | tf_op jit(solution)/shard_map/ppermute | solution.py:34
  64.4 38.2 %collective-permute-start.5 = (bf16[5,640,128]{2,1,0:T(8,128)(2,1)}, bf16[5,640,128]{2,1,0:T(8,128)(2,1)S(1)}, u32[]{:S(2)}, u32[]{:S(2)}) collective-permute-start(bf16[5,640,128]{2,1,0:T(8,128)(2,1)} %get-tuple-element.28), channel_id=1, source_target_pairs={{0,32},{4,36},{8,40},{12,44},{16,48},{20,52},{24,56},{28,60},{32,0... | collective-permute-start | bytes 2457608 | tf_op jit(solution)/shard_map/ppermute | solution.py:34
  67.1 35.5 %collective-permute-start.6 = (bf16[5,640,128]{2,1,0:T(8,128)(2,1)}, bf16[5,640,128]{2,1,0:T(8,128)(2,1)S(1)}, u32[]{:S(2)}, u32[]{:S(2)}) collective-permute-start(bf16[5,640,128]{2,1,0:T(8,128)(2,1)} %get-tuple-element.29), channel_id=1, source_target_pairs={{0,48},{4,52},{8,56},{12,60},{16,0},{20,4},{24,8},{28,12},{32,16},... | collective-permute-start | bytes 2457608 | tf_op jit(solution)/shard_map/ppermute | solution.py:34
  84.5 18.1 %copy-start.10 = (bf16[5,640,128]{2,1,0:T(8,128)(2,1)}, bf16[5,640,128]{2,1,0:T(8,128)(2,1)S(1)}, u32[]{:S(2)}) copy-start(bf16[5,640,128]{2,1,0:T(8,128)(2,1)S(1)} %collective-permute-done.4.t1) | copy-start | bytes 2457604
  102.6 0.9 copy-start.11
  102.6 1.2 copy-start.12
  118.6 9.4 %collective-permute-start.7 = (bf16[640,128]{1,0:T(8,128)(2,1)}, bf16[640,128]{1,0:T(8,128)(2,1)S(1)}, u32[]{:S(2)}, u32[]{:S(2)}) collective-permute-start(bf16[640,128]{1,0:T(8,128)(2,1)} %get-tuple-element.32), channel_id=1, source_target_pairs={{0,48},{4,52},{8,56},{12,60},{16,0},{20,4},{24,8},{28,12},{32,16},... | collective-permute-start | bytes 491528 | tf_op jit(solution)/shard_map/ppermute | solution.py:34
  120.6 8.8 %collective-permute-start.8 = (bf16[640,128]{1,0:T(8,128)(2,1)}, bf16[640,128]{1,0:T(8,128)(2,1)S(1)}, u32[]{:S(2)}, u32[]{:S(2)}) collective-permute-start(bf16[640,128]{1,0:T(8,128)(2,1)} %get-tuple-element.33), channel_id=1, source_target_pairs={{0,32},{4,36},{8,40},{12,44},{16,48},{20,52},{24,56},{28,60},{32,0... | collective-permute-start | bytes 491528 | tf_op jit(solution)/shard_map/ppermute | solution.py:34
  121.8 9.8 %collective-permute-start.9 = (bf16[640,128]{1,0:T(8,128)(2,1)}, bf16[640,128]{1,0:T(8,128)(2,1)S(1)}, u32[]{:S(2)}, u32[]{:S(2)}) collective-permute-start(bf16[640,128]{1,0:T(8,128)(2,1)} %get-tuple-element.34), channel_id=1, source_target_pairs={{0,16},{4,20},{8,24},{12,28},{16,32},{20,36},{24,40},{28,44},{32,4... | collective-permute-start | bytes 491528 | tf_op jit(solution)/shard_map/ppermute | solution.py:34
  128.1 3.4 %copy-start.6 = (bf16[640,128]{1,0:T(8,128)(2,1)}, bf16[640,128]{1,0:T(8,128)(2,1)S(1)}, u32[]{:S(2)}) copy-start(bf16[640,128]{1,0:T(8,128)(2,1)S(1)} %collective-permute-done.7.o1) | copy-start | bytes 491524
  129.4 2.1 %copy-start.7 = (bf16[640,128]{1,0:T(8,128)(2,1)}, bf16[640,128]{1,0:T(8,128)(2,1)S(1)}, u32[]{:S(2)}) copy-start(bf16[640,128]{1,0:T(8,128)(2,1)S(1)} %collective-permute-done.8.o2) | copy-start | bytes 491524
  134.4 19.7 %collective-permute-start.10 = (bf16[160,640]{1,0:T(8,128)(2,1)}, bf16[160,640]{1,0:T(8,128)(2,1)S(1)}, u32[]{:S(2)}, u32[]{:S(2)}) collective-permute-start(bf16[160,640]{1,0:T(8,128)(2,1)} %get-tuple-element.36), channel_id=1, source_target_pairs={{0,64},{4,68},{8,72},{12,76},{16,80},{20,84},{24,88},{28,92},{32,9... | collective-permute-start | bytes 614408 | tf_op jit(solution)/shard_map/ppermute | solution.py:48
  134.4 31.8 %collective-permute-start.11 = (bf16[160,640]{1,0:T(8,128)(2,1)}, bf16[160,640]{1,0:T(8,128)(2,1)S(1)}, u32[]{:S(2)}, u32[]{:S(2)}) collective-permute-start(bf16[160,640]{1,0:T(8,128)(2,1)} %get-tuple-element.37), channel_id=1, source_target_pairs={{0,76},{4,64},{8,68},{12,72},{16,92},{20,80},{24,84},{28,88},{32,1... | collective-permute-start | bytes 614408 | tf_op jit(solution)/shard_map/ppermute | solution.py:48
  148.2 19.1 %collective-permute-start.12 = (bf16[160,640]{1,0:T(8,128)(2,1)}, bf16[160,640]{1,0:T(8,128)(2,1)S(1)}, u32[]{:S(2)}, u32[]{:S(2)}) collective-permute-start(bf16[160,640]{1,0:T(8,128)(2,1)} %get-tuple-element.38), channel_id=1, source_target_pairs={{0,72},{4,76},{8,64},{12,68},{16,88},{20,92},{24,80},{28,84},{32,1... | collective-permute-start | bytes 614408 | tf_op jit(solution)/shard_map/ppermute | solution.py:48
  150.2 17.1 %collective-permute-start.13 = (bf16[160,640]{1,0:T(8,128)(2,1)}, bf16[160,640]{1,0:T(8,128)(2,1)S(1)}, u32[]{:S(2)}, u32[]{:S(2)}) collective-permute-start(bf16[160,640]{1,0:T(8,128)(2,1)} %get-tuple-element.39), channel_id=1, source_target_pairs={{0,68},{4,72},{8,76},{12,64},{16,84},{20,88},{24,92},{28,80},{32,1... | collective-permute-start | bytes 614408 | tf_op jit(solution)/shard_map/ppermute | solution.py:48
  154.1 13.2 %copy-start.2 = (bf16[160,640]{1,0:T(8,128)(2,1)}, bf16[160,640]{1,0:T(8,128)(2,1)S(1)}, u32[]{:S(2)}) copy-start(bf16[160,640]{1,0:T(8,128)(2,1)S(1)} %collective-permute-done.10.a0) | copy-start | bytes 614404
  166.2 1.1 copy-start.3
  171.4 5.0 %collective-permute-start.14 = (f32[20,128]{1,0:T(8,128)S(1)}, f32[20,128]{1,0:T(8,128)S(1)}, u32[]{:S(2)}, u32[]{:S(2)}) collective-permute-start(f32[20,128]{1,0:T(8,128)S(1)} %bitcast.34), channel_id=1, source_target_pairs={{0,16},{4,20},{8,24},{12,28},{16,32},{20,36},{24,40},{28,44},{32,4... | collective-permute-start | bytes 30728 | tf_op jit(solution)/shard_map/ppermute | solution.py:34
  171.5 5.3 %collective-permute-start.15 = (f32[20,128]{1,0:T(8,128)S(1)}, f32[20,128]{1,0:T(8,128)S(1)}, u32[]{:S(2)}, u32[]{:S(2)}) collective-permute-start(f32[20,128]{1,0:T(8,128)S(1)} %bitcast.35), channel_id=1, source_target_pairs={{0,32},{4,36},{8,40},{12,44},{16,48},{20,52},{24,56},{28,60},{32,0... | collective-permute-start | bytes 30728 | tf_op jit(solution)/shard_map/ppermute | solution.py:34
  173.7 3.7 %collective-permute-start.16 = (f32[20,128]{1,0:T(8,128)S(1)}, f32[20,128]{1,0:T(8,128)S(1)}, u32[]{:S(2)}, u32[]{:S(2)}) collective-permute-start(f32[20,128]{1,0:T(8,128)S(1)} %bitcast.36), channel_id=1, source_target_pairs={{0,48},{4,52},{8,56},{12,60},{16,0},{20,4},{24,8},{28,12},{32,16},... | collective-permute-start | bytes 30728 | tf_op jit(solution)/shard_map/ppermute | solution.py:34
  177.4 5.5 %collective-permute-start.17 = (f32[20,128]{1,0:T(8,128)S(1)}, f32[20,128]{1,0:T(8,128)S(1)}, u32[]{:S(2)}, u32[]{:S(2)}) collective-permute-start(f32[20,128]{1,0:T(8,128)S(1)} %add_add_fusion.1), channel_id=1, source_target_pairs={{0,4},{4,8},{8,12},{12,0},{16,20},{20,24},{24,28},{28,16},{32,36},... | collective-permute-start | bytes 30728 | tf_op jit(solution)/shard_map/ppermute | solution.py:29
  179.9 4.6 %collective-permute-start.18 = (f32[20,128]{1,0:T(8,128)S(1)}, f32[20,128]{1,0:T(8,128)S(1)}, u32[]{:S(2)}, u32[]{:S(2)}) collective-permute-start(f32[20,128]{1,0:T(8,128)S(1)} %add_add_fusion.1), channel_id=1, source_target_pairs={{0,8},{4,12},{8,0},{12,4},{16,24},{20,28},{24,16},{28,20},{32,40},... | collective-permute-start | bytes 30728 | tf_op jit(solution)/shard_map/ppermute | solution.py:29
  181.9 3.7 %collective-permute-start.19 = (f32[20,128]{1,0:T(8,128)S(1)}, f32[20,128]{1,0:T(8,128)S(1)}, u32[]{:S(2)}, u32[]{:S(2)}) collective-permute-start(f32[20,128]{1,0:T(8,128)S(1)} %add_add_fusion.1), channel_id=1, source_target_pairs={{0,12},{4,0},{8,4},{12,8},{16,28},{20,16},{24,20},{28,24},{32,44},... | collective-permute-start | bytes 30728 | tf_op jit(solution)/shard_map/ppermute | solution.py:29
  185.6 5.1 %collective-permute-start.20 = (f32[21,128]{1,0:T(8,128)S(1)}, f32[21,128]{1,0:T(8,128)S(1)}, u32[]{:S(2)}, u32[]{:S(2)}) collective-permute-start(f32[21,128]{1,0:T(8,128)S(1)} %concatenate.15), channel_id=1, source_target_pairs={{0,1},{1,2},{2,3},{3,0},{4,5},{5,6},{6,7},{7,4},{8,9},{9,10},{10,1... | collective-permute-start | bytes 32264 | tf_op jit(solution)/shard_map/ppermute | solution.py:38
  187.2 5.2 %collective-permute-start.21 = (f32[21,128]{1,0:T(8,128)S(1)}, f32[21,128]{1,0:T(8,128)S(1)}, u32[]{:S(2)}, u32[]{:S(2)}) collective-permute-start(f32[21,128]{1,0:T(8,128)S(1)} %concatenate.15), channel_id=1, source_target_pairs={{0,2},{1,3},{2,0},{3,1},{4,6},{5,7},{6,4},{7,5},{8,10},{9,11},{10,... | collective-permute-start | bytes 32264 | tf_op jit(solution)/shard_map/ppermute | solution.py:38
  188.2 4.8 %collective-permute-start.22 = (f32[21,128]{1,0:T(8,128)S(1)}, f32[21,128]{1,0:T(8,128)S(1)}, u32[]{:S(2)}, u32[]{:S(2)}) collective-permute-start(f32[21,128]{1,0:T(8,128)S(1)} %concatenate.15), channel_id=1, source_target_pairs={{0,3},{1,0},{2,1},{3,2},{4,7},{5,4},{6,5},{7,6},{8,11},{9,8},{10,9... | collective-permute-start | bytes 32264 | tf_op jit(solution)/shard_map/ppermute | solution.py:38
  (4 other events, 2.7 us)
